TPU v7x, 32 devices: a whole 2x2x4 slice. The times are simulated.
32 devices in a mesh: req: 8 (over z, y), grp: 4 (over x, core).
Axes of the slice: x: 2, y: 2, z: 4, core: 2. Of those that a mesh axis runs over, the one named last changes fastest.
Arguments:
- hidden_in: bfloat16 [16384, 1280], P(('req', 'grp')), may hold values from -28 to 28
- queries: bfloat16 [16384, 1280], P(('req', 'grp')), may hold values from -20 to 20
- projected_keys: bfloat16 [16384, 320], P(('req', 'grp')), may hold values from -20 to 20
- projected_values: bfloat16 [16384, 320], P(('req', 'grp')), may hold values from -6 to 6
- segment: int32 [8, 4, 512], P('req', 'grp'), may hold values from 0 to 511, as said below
- live_rows: int32 [8, 4], P('req', 'grp'), may hold values from 0 to 512, as said below
- out_weight: bfloat16 [1280, 1280], replicated, may hold values from -0.15625 to 0.15625
- norm_gain: float32 [1280], replicated, may hold values from 0.5 to 1.5
- gate_weight: bfloat16 [1280, 3584], P(None, 'grp'), may hold values from -0.15625 to 0.15625
- up_weight: bfloat16 [1280, 3584], P(None, 'grp'), may hold values from -0.15625 to 0.15625
- down_weight: bfloat16 [3584, 1280], P('grp'), may hold values from -0.09375 to 0.09375
Outputs:
- layer_out: bfloat16 [16384, 1280], P(('req', 'grp'))
Inputs may be any that keep to these rules, and one draw needn't show every extreme that they name: `live_rows`: in each group (one index of grp) the live rows of the 8 owners sum to exactly 1024, and one owner of each group has all 512 slots live. `segment`: within one owner the ids start at 0 at its first slot and rise by 0 or 1 from slot to slot.
All inputs are finite; a program needn't handle non-finite values.
Results may differ from a plain program's by a relative error of at most 0.008.
Values may be sent and summed in bfloat16 or wider, within the bound.
A program may use at most 128 MiB of HBM per device.

v0:
```python
import math

import jax
import jax.numpy as jnp
from jax import lax
from jax.sharding import PartitionSpec as P

QUERY_HEADS = 20
KEY_VALUE_HEADS = 5
HEAD_SIZE = 64
WINDOW = 128
SINK = 4
BAL = 128


rope_base = 10000.0
norm_eps = 1e-05


def apply_rotary(table, token_position):
    half = table.shape[-1] // 2
    inverse = rope_base ** (-(2.0 * jnp.arange(half, dtype=jnp.float32)) / table.shape[-1])
    angle = token_position.astype(jnp.float32)[:, None] * inverse[None, :]
    cosine = jnp.concatenate([jnp.cos(angle), jnp.cos(angle)], axis=-1)[:, None, :]
    sine = jnp.concatenate([jnp.sin(angle), jnp.sin(angle)], axis=-1)[:, None, :]
    numbers = table.astype(jnp.float32)
    turned = jnp.concatenate([-numbers[..., half:], numbers[..., :half]], axis=-1)
    return numbers * cosine + turned * sine


def attend(queries, projected_keys, projected_values, segment):
    slot_capacity = queries.shape[0]
    slots = jnp.arange(slot_capacity, dtype=jnp.int32)
    begins = jnp.concatenate([jnp.ones((1,), dtype=jnp.bool_), segment[1:] != segment[:-1]])
    starts = lax.cummax(jnp.where(begins, slots, 0), axis=0)
    token_position = slots - starts
    head_group = QUERY_HEADS // KEY_VALUE_HEADS
    query_rotated = (
        apply_rotary(queries.reshape(slot_capacity, QUERY_HEADS, HEAD_SIZE), token_position)
        .astype(jnp.bfloat16)
        .reshape(slot_capacity, KEY_VALUE_HEADS, head_group, HEAD_SIZE)
    )
    key_rotated = apply_rotary(
        projected_keys.reshape(slot_capacity, KEY_VALUE_HEADS, HEAD_SIZE), token_position
    ).astype(jnp.bfloat16)
    scores = jnp.einsum(
        "qngd,knd->ngqk", query_rotated, key_rotated, preferred_element_type=jnp.float32
    ) / math.sqrt(HEAD_SIZE)
    allowed = (segment[:, None] == segment[None, :]) & (slots[None, :] <= slots[:, None])
    allowed = allowed & (
        (slots[:, None] - slots[None, :] < WINDOW) | (token_position[None, :] < SINK)
    )
    scores = jnp.where(allowed, scores, -jnp.inf)
    largest = jnp.max(scores, axis=-1, keepdims=True)
    raised = jnp.exp(scores - largest)
    layer_weights = (raised / jnp.sum(raised, axis=-1, keepdims=True)).astype(jnp.bfloat16)
    attended_context = jnp.einsum(
        "hemz,zhc->mhec",
        layer_weights,
        projected_values.reshape(slot_capacity, KEY_VALUE_HEADS, HEAD_SIZE),
        preferred_element_type=jnp.float32,
    )
    return attended_context.reshape(slot_capacity, QUERY_HEADS * HEAD_SIZE).astype(jnp.bfloat16)


def normalize(rows, norm_gain):
    numbers = rows.astype(jnp.float32)
    factor = lax.rsqrt(jnp.mean(numbers * numbers, axis=-1, keepdims=True) + norm_eps)
    return (numbers * factor * norm_gain[None, :]).astype(jnp.bfloat16)


def project(attended_context, hidden_in, out_weight):
    return (
        hidden_in.astype(jnp.float32)
        + jnp.dot(attended_context, out_weight, preferred_element_type=jnp.float32)
    ).astype(jnp.bfloat16)


def feed_forward(normed, gate_weight, up_weight, down_weight):
    gathered = lax.all_gather(normed, "grp", axis=0, tiled=True)
    gate = jnp.dot(gathered, gate_weight, preferred_element_type=jnp.float32)
    upward = jnp.dot(gathered, up_weight, preferred_element_type=jnp.float32)
    hidden = (jax.nn.silu(gate) * upward).astype(jnp.bfloat16)
    return lax.psum_scatter(
        jnp.dot(hidden, down_weight, preferred_element_type=jnp.float32).astype(jnp.bfloat16),
        "grp",
        scatter_dimension=0,
        tiled=True,
    ).astype(jnp.float32)


def on_device(
    hidden_in,
    queries,
    projected_keys,
    projected_values,
    segment,
    live_rows,
    out_weight,
    norm_gain,
    gate_weight,
    up_weight,
    down_weight,
):
    slot_capacity = hidden_in.shape[0]
    attended_context = attend(
        queries, projected_keys, projected_values, segment.reshape(slot_capacity)
    )
    slots = jnp.arange(slot_capacity, dtype=jnp.int32)
    own_count = live_rows.reshape(())
    request_owners = lax.axis_size("req")
    own_index = lax.axis_index("req")
    block_rows = slot_capacity // request_owners
    counts = lax.all_gather(live_rows.reshape(1), "req", axis=0, tiled=True)
    ends = jnp.cumsum(counts)
    firsts = ends - counts
    owner_ids = jnp.arange(request_owners, dtype=jnp.int32)
    own_first = jnp.sum(jnp.where(owner_ids == own_index, firsts, 0))
    own_shift = own_first % request_owners
    keep = slots < own_count
    stream = jnp.arange(BAL, dtype=jnp.int32) * request_owners + own_index
    source = jnp.sum((ends[None, :] <= stream[:, None]).astype(jnp.int32), axis=1)
    source_first = jnp.sum(
        jnp.where(source[:, None] == owner_ids[None, :], firsts[None, :], 0), axis=1
    )
    pick = (stream - source_first) // request_owners * request_owners + source
    rows = project(attended_context, hidden_in, out_weight)
    kept = jnp.where(keep[:, None], rows, jnp.zeros_like(rows))
    arrived = lax.all_to_all(
        jnp.roll(kept.reshape(block_rows, request_owners, rows.shape[1]), own_shift, axis=1),
        "req",
        split_axis=1,
        concat_axis=1,
        tiled=True,
    )
    mixed = arrived.reshape(slot_capacity, -1)[pick]
    normed = normalize(mixed, norm_gain)
    result = (
        mixed.astype(jnp.float32) + feed_forward(normed, gate_weight, up_weight, down_weight)
    ).astype(jnp.bfloat16)
    lanes = (own_index - firsts) % request_owners
    source_row = jnp.arange(block_rows, dtype=jnp.int32)[:, None] * request_owners + lanes[None, :]
    valid = source_row < counts[None, :]
    target = jnp.where(valid, (firsts[None, :] + source_row) // request_owners, 0)
    outgoing = jnp.where(valid[:, :, None], result[target], jnp.zeros((), jnp.bfloat16))
    returned = lax.all_to_all(outgoing, "req", split_axis=1, concat_axis=1, tiled=True)
    return jnp.roll(returned, -own_shift, axis=1).reshape(slot_capacity, -1)


def solution(mesh):
    placed = (
        P(("req", "grp"), None),
        P(("req", "grp"), None),
        P(("req", "grp"), None),
        P(("req", "grp"), None),
        P("req", "grp", None),
        P("req", "grp"),
        P(),
        P(),
        P(None, "grp"),
        P(None, "grp"),
        P("grp", None),
    )
    return jax.shard_map(
        on_device, mesh=mesh, in_specs=placed, out_specs=P(("req", "grp"), None), check_vma=False
    )
```

profile of v0, /device:TPU:0, one launch (start us, length us, event | category | flops | bytes accessed | tf_op | source)
XLA Modules:
  0.0 226.0 jit_solution(4414300845254375304)
XLA Ops:
  6.5 0.0 copy-start
  7.3 1.4 dynamic-slice
  8.8 0.7 bitcast_dynamic-update-slice_fusion
  9.4 13.1 %all-reduce = s32[8]{0:T(128)S(1)} all-reduce(s32[8]{0:T(128)S(1)} %bitcast_dynamic-update-slice_fusion), channel_id=2, replica_groups=mesh['req'=8,'grp'=4] {'req'}, use_global_device_ids=true, to_apply=%add | all-reduce | flops 8 | bytes 64 | tf_op jit(solution)/shard_map/all_gather | solution.py:114
  22.5 0.2 reduce-window.19
  22.7 0.6 fusion.37
  25.3 0.5 multiply_power_fusion
  25.8 0.8 compare_reduce_fusion
  26.7 0.1 add_select_fusion.1
  26.8 0.3 reduce-window.20
  27.1 0.1 slice.29
  27.2 0.1 slice_reduce_fusion
  27.3 0.7 fusion.36
  28.0 0.1 fusion.35
  28.1 1.7 slice.40
  29.8 1.9 convert.3
  31.7 2.4 %copy.32 = bf16[512,1280]{0,1:T(8,128)(2,1)} copy(bf16[512,1280]{1,0:T(8,128)(2,1)} %param.14) | data formatting | bytes 2621440 | tf_op args[1]
  34.1 1.7 convert_element_type.96
  35.8 0.0 copy-start.1
  35.8 0.0 copy-start.2
  35.8 0.0 copy-start.3
  35.8 1.8 slice_negate_fusion
  37.6 0.6 copy-done.1
  38.2 0.0 copy-done.2
  38.2 0.8 slice_negate_fusion.1
  39.0 0.5 iota_compare_fusion.2
  39.5 0.0 copy-done.5
  39.5 0.3 fusion.18
  39.8 0.3 multiply_cosine_fusion
  40.1 0.7 pad_maximum_fusion
  40.8 13.8 %fusion.43 = (f32[5,4,512]{2,1,0:T(4,128)}, f32[5,4,512,512]{2,3,1,0:T(8,128)}) fusion(pred[512,512]{0,1:T(8,128)(4,1)S(1)} %fusion.18, f32[512,5,4,32]{0,3,2,1:T(8,128)} %bitcast.85, f32[512,5,4,32]{0,3,2,1:T(8,128)} %bitcast.84, f32[512,5,4,64]{0,3,2,1:T(8,128)} %bitcast.82, f32[512,64]{0,1:T(8,128)} %get-tuple-element.15, ...), kind=kOutput, calls=%fused_computation.105 | convolution fusion | flops 696320512 | bytes 27762688 | tf_op jit(solution)/shard_map/sub | solution.py:55
  54.6 9.0 %fusion.13 = bf16[5,4,512,64]{2,3,1,0:T(8,128)(2,1)S(1)} fusion(bf16[512,5,64,1]{0,2,3,1:T(8,128)(2,1)} %bitcast.92, f32[5,4,512,512]{2,3,1,0:T(8,128)} %get-tuple-element.13, f32[5,4,512]{2,1,0:T(4,128)} %get-tuple-element.12), kind=kOutput, calls=%fused_computation.25 | convolution fusion | flops 682229760 | bytes 22650880 | tf_op jit(solution)/shard_map/hemz,zhc->mhec/dot_general | solution.py:57
  63.6 0.0 copy-done
  63.6 0.0 copy-done.9
  63.6 0.0 copy-done.10
  63.6 2.0 fusion.8
  65.6 1.3 copy.34
  66.9 2.9 %fusion.16 = bf16[64,8,1280]{2,0,1:T(8,128)(2,1)} fusion(s32[]{:T(128)S(6)} %select_n.118, bf16[64,8,1280]{2,0,1:T(8,128)(2,1)} %copy.34), kind=kLoop, calls=%fused_computation.28 | loop fusion | flops 655360 | bytes 2621444 | tf_op jit(solution)/shard_map/jit(_roll_dynamic)/concatenate | solution.py:130
  69.8 4.4 %all-to-all-start = ((bf16[64,8,1280]{2,0,1:T(8,128)(2,1)}), bf16[64,8,1280]{2,0,1:T(8,128)(2,1)}, u32[]{:S(2)}, u32[]{:S(2)}) async-start(bf16[64,8,1280]{2,0,1:T(8,128)(2,1)} %fusion.16), calls=%async_computation | async-start | bytes 2621440 | tf_op jit(solution)/shard_map/all_to_all | solution.py:129
  74.2 0.2 all-gather.3.cloned.1.call-start
  74.4 0.1 convert_reduce_fusion
  74.5 0.1 select_reduce_fusion
  74.6 28.5 %all-to-all-done = bf16[64,8,1280]{2,0,1:T(8,128)(2,1)} async-done(((bf16[64,8,1280]{2,0,1:T(8,128)(2,1)}), bf16[64,8,1280]{2,0,1:T(8,128)(2,1)}, u32[]{:S(2)}, u32[]{:S(2)}) %all-to-all-start) | async-done | bytes 1310752 | tf_op jit(solution)/shard_map/all_to_all | solution.py:129
  103.1 3.1 %copy.45 = bf16[64,8,1280]{2,1,0:T(8,128)(2,1)} copy(bf16[64,8,1280]{2,0,1:T(8,128)(2,1)} %all-to-all-done) | data formatting | bytes 2621440 | tf_op jit(solution)/shard_map/all_to_all | solution.py:129
  106.2 3.4 %gather_fusion = bf16[128,1280]{1,0:T(8,128)(2,1)} fusion(bf16[512,1280]{1,0:T(8,128)(2,1)} %bitcast.80, s32[1024]{0:T(1024)S(1)} %pad_clamp_fusion.1), kind=kCustom, calls=%fused_computation | custom fusion | bytes 655872 | tf_op jit(solution)/shard_map/gather | solution.py:136
  109.6 1.1 fusion.20
  110.7 1.8 fusion.22
  112.6 0.0 all-gather.3.cloned.1.call-update
  112.6 0.0 reduce-scatter.2.cloned.1.call-start
  112.6 17.1 %all-gather.3.cloned.1.call-done = bf16[512,1280]{1,0:T(8,128)(2,1)} async-done(((bf16[128,1280]{1,0:T(8,128)(2,1)}), bf16[512,1280]{1,0:T(8,128)(2,1)}) %all-gather.3.cloned.1.call-update) | async-done | bytes 1310736 | tf_op jit(solution)/shard_map/all_gather | solution.py:80
  129.8 4.8 %fusion.50 = f32[512,896]{1,0:T(8,128)} fusion(bf16[512,1280]{1,0:T(8,128)(2,1)} %all-gather.3.cloned.1.call-done, bf16[1280,896]{1,0:T(8,128)(2,1)} %param.21), kind=kOutput, calls=%fused_computation.106 | convolution fusion | flops 1174405120 | bytes 5439488 | tf_op jit(solution)/shard_map/dot_general | solution.py:81
  134.6 7.3 %convolution_convert_fusion = bf16[512,1280]{1,0:T(8,128)(2,1)} fusion(bf16[896,1280]{1,0:T(8,128)(2,1)} %param.23, f32[512,896]{1,0:T(8,128)} %fusion.50, bf16[512,1280]{1,0:T(8,128)(2,1)} %all-gather.3.cloned.1.call-done, bf16[1280,896]{1,0:T(8,128)(2,1)} %param.22), kind=kOutput, calls=%fused_computation.13 | convolution fusion | flops 2352218112 | bytes 9043968 | tf_op jit(solution)/shard_map/dot_general | solution.py:85
  142.0 0.0 reduce-scatter.2.cloned.1.call-update
  142.0 0.1 compare_select_fusion
  142.1 0.1 reshape.412
  142.2 0.1 add_compare_fusion.1
  142.3 26.4 %reduce-scatter.2.cloned.1.call-done = bf16[128,1280]{1,0:T(8,128)(2,1)} async-done(((bf16[512,1280]{1,0:T(8,128)(2,1)}), bf16[128,1280]{1,0:T(8,128)(2,1)}) %reduce-scatter.2.cloned.1.call-update) | async-done | bytes 327696 | tf_op jit(solution)/shard_map/reduce_scatter | solution.py:84
  168.7 1.9 fusion.23
  170.5 4.9 %gather_fusion.1 = bf16[512,1280]{1,0:T(8,128)(2,1)} fusion(bf16[128,1280]{1,0:T(8,128)(2,1)} %fusion.23, s32[1024]{0:T(1024)S(1)} %pad_clamp_fusion), kind=kCustom, calls=%fused_computation.1 | custom fusion | bytes 2623488 | tf_op jit(solution)/shard_map/gather | solution.py:145
  175.5 2.7 %copy_select_fusion = bf16[64,8,1280]{2,0,1:T(8,128)(2,1)} fusion(bf16[64,8,1280]{2,1,0:T(8,128)(2,1)} %bitcast.83, pred[64,8]{0,1:T(8,128)(4,1)S(1)} %add_compare_fusion.1), kind=kLoop, calls=%fused_computation.30 | loop fusion | flops 655360 | bytes 2621952 | tf_op jit(solution)/shard_map/jit(_where)/select_n | solution.py:145
  178.1 5.5 %all-to-all-start.1 = ((bf16[64,8,1280]{2,0,1:T(8,128)(2,1)}), bf16[64,8,1280]{2,0,1:T(8,128)(2,1)}, u32[]{:S(2)}, u32[]{:S(2)}) async-start(bf16[64,8,1280]{2,0,1:T(8,128)(2,1)} %copy_select_fusion), calls=%async_computation.2 | async-start | bytes 2621440 | tf_op jit(solution)/shard_map/all_to_all | solution.py:146
  183.7 31.5 %all-to-all-done.1 = bf16[64,8,1280]{2,0,1:T(8,128)(2,1)} async-done(((bf16[64,8,1280]{2,0,1:T(8,128)(2,1)}), bf16[64,8,1280]{2,0,1:T(8,128)(2,1)}, u32[]{:S(2)}, u32[]{:S(2)}) %all-to-all-start.1) | async-done | bytes 1310752 | tf_op jit(solution)/shard_map/all_to_all | solution.py:146
  215.2 2.0 copy.38
  217.2 2.0 fusion.15
  (21 shorter events, 0.1 us)
Async XLA Ops:
  6.5 57.1 %copy-start = (bf16[1280,1280]{1,0:T(8,128)(2,1)S(1)}, bf16[1280,1280]{1,0:T(8,128)(2,1)}, u32[]{:S(2)}) copy-start(bf16[1280,1280]{1,0:T(8,128)(2,1)} %param.19) | copy-start | bytes 9830404
  22.7 4.0 %copy-start.7 = (s32[8,1]{0,1:T(1,128)}, s32[8,1]{0,1:T(1,128)S(1)}, u32[]{:S(2)}) copy-start(s32[8,1]{0,1:T(1,128)S(1)} %reduce-window.19) | copy-start | bytes 100
  35.8 2.4 %copy-start.1 = (f32[512,1280]{0,1:T(8,128)}, f32[512,1280]{0,1:T(8,128)S(1)}, u32[]{:S(2)}) copy-start(f32[512,1280]{0,1:T(8,128)S(1)} %convert_element_type.96) | copy-start | bytes 7864324
  35.8 2.4 %copy-start.2 = (f32[512,5,64]{0,2,1:T(8,128)S(1)}, f32[512,5,64]{0,2,1:T(8,128)}, u32[]{:S(2)}) copy-start(f32[512,5,64]{0,2,1:T(8,128)} %convert.3) | copy-start | bytes 1966084
  35.8 3.7 %copy-start.3 = (s32[1,1,512]{2,1,0:T(1,128)S(1)}, s32[1,1,512]{2,1,0:T(1,128)}, u32[]{:S(2)}) copy-start(s32[1,1,512]{2,1,0:T(1,128)} %param.17) | copy-start | bytes 6148
  35.8 3.7 %copy-start.5 = (pred[512]{0:T(512)(128)(4,1)S(1)}, pred[512]{0:T(512)(128)(4,1)}, u32[]{:S(2)}) copy-start(pred[512]{0:T(512)(128)(4,1)} %fusion.36) | copy-start | bytes 1540
  35.8 4.0 %copy-start.6 = (f32[32]{0:T(128)S(1)}, f32[32]{0:T(128)}, u32[]{:S(2)}) copy-start(f32[32]{0:T(128)} %multiply_power_fusion) | copy-start | bytes 388
  54.6 9.0 %copy-start.9 = (bf16[512,1280]{1,0:T(8,128)(2,1)S(1)}, bf16[512,1280]{1,0:T(8,128)(2,1)}, u32[]{:S(2)}) copy-start(bf16[512,1280]{1,0:T(8,128)(2,1)} %param.13) | copy-start | bytes 3932164
  54.6 9.0 %copy-start.10 = (pred[512]{0:T(512)(128)(4,1)S(1)}, pred[512]{0:T(512)(128)(4,1)}, u32[]{:S(2)}) copy-start(pred[512]{0:T(512)(128)(4,1)} %iota_compare_fusion.2) | copy-start | bytes 1540
  69.8 4.6 %copy-start.8 = (s32[8,1]{0,1:T(1,128)S(1)}, s32[8,1]{0,1:T(1,128)}, u32[]{:S(2)}) copy-start(s32[8,1]{0,1:T(1,128)} %copy-done.7) | copy-start | bytes 100
  69.8 33.4 %all-to-all-start = ((bf16[64,8,1280]{2,0,1:T(8,128)(2,1)}), bf16[64,8,1280]{2,0,1:T(8,128)(2,1)}, u32[]{:S(2)}, u32[]{:S(2)}) async-start(bf16[64,8,1280]{2,0,1:T(8,128)(2,1)} %fusion.16), calls=%async_computation | async-start | bytes 2621440 | tf_op jit(solution)/shard_map/all_to_all | solution.py:129
  74.2 55.6 %all-gather.3.cloned.1.call-start = ((), (), s32[]{:S(2)}) async-start(), calls=%async_computation.3 | async-start | bytes 1638400 | tf_op jit(solution)/shard_map/all_gather | solution.py:80
  106.2 4.5 %copy-start.4 = (f32[1280]{0:T(1024)S(1)}, f32[1280]{0:T(1024)}, u32[]{:S(2)}) copy-start(f32[1280]{0:T(1024)} %param.20) | copy-start | bytes 15364
  112.6 56.1 %reduce-scatter.2.cloned.1.call-start = ((), (), s32[]{:S(2)}) async-start(), calls=%async_computation.4 | async-start | bytes 1638400 | tf_op jit(solution)/shard_map/reduce_scatter | solution.py:84
  178.1 37.0 %all-to-all-start.1 = ((bf16[64,8,1280]{2,0,1:T(8,128)(2,1)}), bf16[64,8,1280]{2,0,1:T(8,128)(2,1)}, u32[]{:S(2)}, u32[]{:S(2)}) async-start(bf16[64,8,1280]{2,0,1:T(8,128)(2,1)} %copy_select_fusion), calls=%async_computation.2 | async-start | bytes 2621440 | tf_op jit(solution)/shard_map/all_to_all | solution.py:146
Sparse Core Ops, SparseCore 0:
  112.7 17.0 all-gather.2
  142.1 26.5 reduce-scatter.1
where the time goes:
time: 227 us; the launch traced here: 226 us
  waiting for transfers between devices  104 us (46%)
  matrix products  36.9 us (16%)
  other arithmetic  24.1 us (11%)
  local copies, waits for them, and re-layouts  21.8 us (10%)
  between operations  16.4 us (7%)
  blocking collectives  13.1 us (6%)
  starting transfers between devices  10.2 us (4%)
    all_to_all x1, waiting for transfers between devices, on_device(): lax.all_to_all(outgoing, 'req', split_axis=1, concat_axis=1, tiled=True)  31.5 us
    all_to_all x1, waiting for transfers between devices, on_device(): lax.all_to_all(jnp.roll(kept.reshape(block_rows, request_owners, rows.sha...  28.5 us
    reduce_scatter x1, waiting for transfers between devices, feed_forward(): lax.psum_scatter(jnp.dot(hidden, down_weight, preferred_element_type=jnp....  26.4 us
    all_gather x1, waiting for transfers between devices, feed_forward(): gathered = lax.all_gather(normed, 'grp', axis=0, tiled=True)  17.1 us
    sub x1, matrix products, attend(): raised = jnp.exp(scores - largest)  13.8 us
    all_gather x1, blocking collectives, on_device(): counts = lax.all_gather(live_rows.reshape(1), 'req', axis=0, tiled=True)  13.1 us
    dot_general x1, matrix products, attend(): jnp.einsum('hemz,zhc->mhec', layer_weights, projected_values.reshape(slot...  9 us
    dot_general x1, matrix products, feed_forward(): jnp.dot(hidden, down_weight, preferred_element_type=jnp.float32)  7.34 us
  transfers between devices with their start and end apart: 4, of which 4 were waited for; matrix products, arithmetic and copies ran while one was open for 0% of the time, Pallas kernels for 0%

commit v1 on v0

v1 whole, which is shorter than its diff:
```python
import functools

import jax
import jax.numpy as jnp
import numpy as np
from jax import lax
from jax.experimental import pallas as pl
from jax.experimental.pallas import tpu as pltpu
from jax.sharding import PartitionSpec as P

QUERY_HEADS = 20
KEY_VALUE_HEADS = 5
HEAD_SIZE = 64
WINDOW = 128
SINK = 4
ROPE_BASE = 10000.0
NORM_EPS = 1e-05

MESH = pl.DeviceIdType.MESH
F32 = jnp.float32
BF16 = jnp.bfloat16
ROWS = 128
LANES = 256
HEAD_GROUP = QUERY_HEADS // KEY_VALUE_HEADS
HIDDEN_TILE = 128
MASKED = -1e30

CORE, ACROSS, FORWARD, SUM_OWN, SUM_DIAG, SUM_ACROSS = range(6)


def rotary_table(slot_capacity):
    half = HEAD_SIZE // 2
    inverse = np.float32(ROPE_BASE) ** (-(2.0 * np.arange(half, dtype=np.float32)) / HEAD_SIZE)
    angle = np.arange(slot_capacity, dtype=np.float32)[:, None] * inverse.astype(np.float32)[None, :]
    cosine = np.tile(np.cos(angle.astype(np.float64)), (1, 4))
    sine = np.tile(np.sin(angle.astype(np.float64)), (1, 4))
    exact = np.concatenate([cosine, sine], axis=1).astype(np.float32)
    terms = []
    for _ in range(3):
        term = exact.astype(jnp.bfloat16)
        terms.append(term)
        exact = exact - term.astype(np.float32)
    return np.concatenate(terms, axis=1)


def dot(a, b):
    return jnp.dot(a, b, preferred_element_type=F32)


def dot_t(a, b):
    return lax.dot_general(a, b, (((1,), (1,)), ((), ())), preferred_element_type=F32)


def kernel(
    blocks,
    live_ref, queries, keys, values, seg_row, seg_col, table, gain, hidden_hbm, ow_hbm, gate_hbm, up_hbm, down_hbm,
    out,
    hidden, ow, wgu, wd, rows, context, turned_keys, wide_values, cosine, sine, mixed, act, part, own,
    own_out, own_in, diag_out, diag_in, across_out, across_in,
    load_sem, send_sem, recv_sem,
):
    me = lax.axis_index("grp")
    sibling = me + 1 - 2 * lax.rem(me, 2)
    partner = lax.rem(me + 2, 4)
    slots = blocks * ROWS
    tiles = ow.shape[0]
    hidden_tiles = wgu.shape[0]

    loads = []

    def load(src, dst):
        copy = pltpu.make_async_copy(src, dst, load_sem.at[len(loads)])
        copy.start()
        loads.append(copy)
        return copy

    ow_loads = [load(ow_hbm.at[:, pl.ds(LANES * t, LANES)], ow.at[t]) for t in range(tiles)]
    ow_loads.append(load(hidden_hbm, hidden))
    ffn_loads = []
    for t in range(hidden_tiles):
        cols = pl.ds(HIDDEN_TILE * t, HIDDEN_TILE)
        ffn_loads.append(load(gate_hbm.at[:, cols], wgu.at[t, :, pl.ds(0, HIDDEN_TILE)]))
        ffn_loads.append(load(up_hbm.at[:, cols], wgu.at[t, :, pl.ds(HIDDEN_TILE, HIDDEN_TILE)]))
    for t in range(tiles):
        ffn_loads.append(load(down_hbm.at[:, pl.ds(LANES * t, LANES)], wd.at[t]))

    barrier = pltpu.get_barrier_semaphore()
    for other in (sibling, partner):
        pl.semaphore_signal(barrier, inc=1, device_id={"grp": other}, device_id_type=MESH)

    def remote(kind, k, src, dst, other):
        return pltpu.make_async_remote_copy(
            src_ref=src, dst_ref=dst, send_sem=send_sem.at[kind, k], recv_sem=recv_sem.at[kind, k],
            device_id={"grp": other}, device_id_type=MESH,
        )

    to_sibling = [remote(CORE, k, rows.at[k, 0], rows.at[k, 1], sibling) for k in range(blocks)]
    to_partner = [remote(ACROSS, k, rows.at[k, 0], rows.at[k, 2], partner) for k in range(blocks)]
    forward = [remote(FORWARD, k, rows.at[k, 2], rows.at[k, 3], sibling) for k in range(blocks)]
    sum_own = [remote(SUM_OWN, k, own_out.at[k], own_in.at[k], sibling) for k in range(blocks)]
    sum_diag = [remote(SUM_DIAG, k, diag_out.at[k], diag_in.at[k], sibling) for k in range(blocks)]
    sum_across = [remote(SUM_ACROSS, k, across_out.at[k], across_in.at[k], partner) for k in range(blocks)]

    same = seg_col[...] == seg_row[...]
    row_ids = lax.broadcasted_iota(jnp.int32, (slots, slots), 0)
    col_ids = lax.broadcasted_iota(jnp.int32, (slots, slots), 1)
    position = jnp.sum(jnp.where(same & (col_ids <= row_ids), 1.0, 0.0), axis=1, keepdims=True) - 1.0
    key_position = jnp.sum(jnp.where(same & (row_ids <= col_ids), 1.0, 0.0), axis=0, keepdims=True) - 1.0
    chosen = jnp.where(position == col_ids.astype(F32), 1.0, 0.0).astype(BF16)
    factors = dot(chosen, table[...])
    factors = factors[:, :256] + (factors[:, 256:512] + factors[:, 512:])
    cosine[...] = factors[:, :128]
    sine[...] = factors[:, 128:]

    swap_i = lax.broadcasted_iota(jnp.int32, (256, 256), 0)
    swap_j = lax.broadcasted_iota(jnp.int32, (256, 256), 1)
    low = lax.rem(swap_j, HEAD_SIZE) < HEAD_SIZE // 2
    swap = jnp.where(low & (swap_i == swap_j + 32), -1.0, jnp.where(~low & (swap_i == swap_j - 32), 1.0, 0.0))
    swap = swap.astype(BF16)

    key_head = keys[:, :256]
    key_cos, key_sin = cosine[...], sine[...]
    wide_cos = jnp.concatenate([key_cos, key_cos], axis=1)
    wide_sin = jnp.concatenate([key_sin, key_sin], axis=1)
    first = (key_head.astype(F32) * wide_cos + dot(key_head, swap) * wide_sin).astype(BF16)
    key_tail = keys[:, 256:]
    tail = (key_tail.astype(F32) * key_cos[:, :64] + dot(key_tail, swap[:64, :64]) * key_sin[:, :64]).astype(BF16)
    ones = jnp.ones((slots, HEAD_SIZE), BF16)
    for n in range(KEY_VALUE_HEADS):
        turned_keys[n] = first[:, 64 * n : 64 * n + 64] if n < 4 else tail
        wide_values[n] = jnp.concatenate([values[:, 64 * n : 64 * n + 64], ones], axis=1)

    def attend(k):
        lo, width = k * ROWS, (k + 1) * ROWS
        block = pl.ds(lo, ROWS)
        q_ids = lax.broadcasted_iota(jnp.int32, (ROWS, width), 0) + lo
        k_ids = lax.broadcasted_iota(jnp.int32, (ROWS, width), 1)
        allowed = (seg_col[block, :] == seg_row[:, :width]) & (k_ids <= q_ids)
        allowed = allowed & ((q_ids - k_ids < WINDOW) | (key_position[:, :width] < SINK))
        bias = jnp.where(allowed, 0.0, MASKED)
        cos_block, sin_block = cosine[block, :], sine[block, :]
        cos_block = jnp.concatenate([cos_block, cos_block], axis=1)
        sin_block = jnp.concatenate([sin_block, sin_block], axis=1)
        for n in range(KEY_VALUE_HEADS):
            q = queries[block, pl.ds(256 * n, 256)]
            q = (q.astype(F32) * cos_block + dot(q, swap) * sin_block).astype(BF16) * BF16(HEAD_SIZE**-0.5)
            q = jnp.concatenate([q[:, 64 * h : 64 * h + 64] for h in range(HEAD_GROUP)], axis=0)
            scores = dot_t(q, turned_keys[n, :width, :])
            scores = scores.reshape(HEAD_GROUP, ROWS, width) + bias[None]
            raised = jnp.exp(scores - jnp.max(scores, axis=-1, keepdims=True))
            raised = raised.reshape(HEAD_GROUP * ROWS, width).astype(BF16)
            result = dot(raised, wide_values[n, :width, :])
            result = result[:, :64] / result[:, 64:]
            context[:, 256 * n : 256 * n + 256] = jnp.concatenate(
                [result[ROWS * h : ROWS * h + ROWS] for h in range(HEAD_GROUP)], axis=1
            ).astype(BF16)

    def project(k):
        block = pl.ds(k * ROWS, ROWS)
        for t in range(tiles):
            cols = pl.ds(LANES * t, LANES)
            mixed[block, cols] = (hidden[block, cols].astype(F32) + dot(context[...], ow[t])).astype(BF16)
        numbers = mixed[block, :].astype(F32)
        factor = lax.rsqrt(jnp.mean(numbers * numbers, axis=-1, keepdims=True) + NORM_EPS)
        rows[k, 0] = (numbers * factor * gain[...]).astype(BF16)

    def feed_forward(k, first_slot):
        def upward(t, carry):
            both = rows[k, first_slot : first_slot + 2].reshape(2 * ROWS, rows.shape[3])
            product = dot(both, wgu[t])
            gate, up = product[:, :HIDDEN_TILE], product[:, HIDDEN_TILE:]
            act[t] = (gate / (1.0 + jnp.exp(-gate)) * up).astype(BF16)
            return carry

        lax.fori_loop(0, hidden_tiles, upward, 0)
        for t in range(tiles):
            hid = jnp.concatenate([act[j] for j in range(hidden_tiles)], axis=1)
            part[:, LANES * t : LANES * t + LANES] = dot(hid, wd[t])

    def start_block(k):
        attend(k)
        if k == 0:
            for copy in ow_loads:
                copy.wait()
        project(k)
        if k == 0:
            pl.semaphore_wait(barrier, 2)
        to_partner[k].start()
        to_sibling[k].start()

    start_block(0)
    for k in range(blocks):
        if k + 1 < blocks:
            start_block(k + 1)
        if k == 0:
            for copy in ffn_loads:
                copy.wait()
        to_sibling[k].wait_recv()
        feed_forward(k, 0)
        own[k] = part[:ROWS, :]
        own_out[k] = part[ROWS:, :].astype(BF16)
        sum_own[k].start()
        to_partner[k].wait_recv()
        forward[k].start()
        forward[k].wait_recv()
        feed_forward(k, 2)
        diag_out[k] = part[ROWS:, :].astype(BF16)
        sum_diag[k].start()
        sum_diag[k].wait_recv()
        across_out[k] = (part[:ROWS, :] + diag_in[k].astype(F32)).astype(BF16)
        sum_across[k].start()

    live = live_ref[0, 0]
    for k in range(blocks):
        sum_own[k].wait_recv()
        sum_across[k].wait_recv()
        block = pl.ds(k * ROWS, ROWS)
        total = own[k] + own_in[k].astype(F32) + across_in[k].astype(F32) + mixed[block, :].astype(F32)
        slot = lax.broadcasted_iota(jnp.int32, total.shape, 0) + k * ROWS
        out[block, :] = jnp.where(slot < live, total, 0.0).astype(BF16)
    for k in range(blocks):
        for copy in (to_sibling[k], to_partner[k], forward[k], sum_own[k], sum_diag[k], sum_across[k]):
            copy.wait_send()


def on_device(
    hidden_in, queries, projected_keys, projected_values, segment, live_rows, out_weight, norm_gain,
    gate_weight, up_weight, down_weight,
):
    slots, width = hidden_in.shape
    units = gate_weight.shape[1]
    blocks, tiles, hidden_tiles = slots // ROWS, width // LANES, units // HIDDEN_TILE
    vmem = pl.BlockSpec(memory_space=pltpu.VMEM)
    hbm = pl.BlockSpec(memory_space=pl.ANY)
    block_bf16 = pltpu.VMEM((blocks, ROWS, width), BF16)
    return pl.pallas_call(
        functools.partial(kernel, blocks),
        out_shape=jax.ShapeDtypeStruct((slots, width), BF16),
        in_specs=[pl.BlockSpec(memory_space=pltpu.SMEM)] + [vmem] * 7 + [hbm] * 5,
        out_specs=vmem,
        scratch_shapes=[
            pltpu.VMEM((slots, width), BF16),
            pltpu.VMEM((tiles, width, LANES), BF16),
            pltpu.VMEM((hidden_tiles, width, 2 * HIDDEN_TILE), BF16),
            pltpu.VMEM((tiles, units, LANES), BF16),
            pltpu.VMEM((blocks, 4, ROWS, width), BF16),
            pltpu.VMEM((ROWS, width), BF16),
            pltpu.VMEM((KEY_VALUE_HEADS, slots, HEAD_SIZE), BF16),
            pltpu.VMEM((KEY_VALUE_HEADS, slots, 2 * HEAD_SIZE), BF16),
            pltpu.VMEM((slots, 128), F32),
            pltpu.VMEM((slots, 128), F32),
            pltpu.VMEM((slots, width), BF16),
            pltpu.VMEM((hidden_tiles, 2 * ROWS, HIDDEN_TILE), BF16),
            pltpu.VMEM((2 * ROWS, width), F32),
            pltpu.VMEM((blocks, ROWS, width), F32),
            block_bf16, block_bf16, block_bf16, block_bf16, block_bf16, block_bf16,
            pltpu.SemaphoreType.DMA((2 * tiles + 2 * hidden_tiles + 1,)),
            pltpu.SemaphoreType.DMA((6, blocks)),
            pltpu.SemaphoreType.DMA((6, blocks)),
        ],
        compiler_params=pltpu.CompilerParams(
            collective_id=0, has_side_effects=True, vmem_limit_bytes=56 * 1024 * 1024
        ),
        name="decoder_layer",
    )(
        live_rows,
        queries,
        projected_keys,
        projected_values,
        segment.reshape(1, slots),
        segment.reshape(slots, 1),
        jnp.asarray(rotary_table(slots)),
        norm_gain.reshape(1, width),
        hidden_in,
        out_weight,
        gate_weight,
        up_weight,
        down_weight,
    )


def solution(mesh):
    placed = (
        P(("req", "grp"), None),
        P(("req", "grp"), None),
        P(("req", "grp"), None),
        P(("req", "grp"), None),
        P("req", "grp", None),
        P("req", "grp"),
        P(),
        P(),
        P(None, "grp"),
        P(None, "grp"),
        P("grp", None),
    )
    return jax.shard_map(
        on_device, mesh=mesh, in_specs=placed, out_specs=P(("req", "grp"), None), check_vma=False
    )
```

time: 227 us -> 80.7 us (0.36)
  waiting for transfers between devices: 104 us -> 0 us
  Pallas kernels: 0 us -> 70.7 us
  matrix products: 36.9 us -> 0 us
  other arithmetic: 24.1 us -> 0 us
  between operations: 16.4 us -> 0.66 us
  blocking collectives: 13.1 us -> 0 us
  local copies, waits for them, and re-layouts: 21.8 us -> 9.06 us
  starting transfers between devices: 10.2 us -> 0 us
    pallas_call x0 -> x1, Pallas kernels: none -> 70.7 us  [on_device(): pl.pallas_call(functools.partial(kernel, blocks), out_shape=jax.ShapeDtyp...]
    all_to_all x2 -> x0, waiting for transfers between devices: 60 us -> none  [the longest x1 31.5 us: on_device(): lax.all_to_all(outgoing, 'req', split_axis=1, concat_axis=1, tiled=True)]
    reduce_scatter x1 -> x0, waiting for transfers between devices: 26.4 us -> none  [feed_forward(): lax.psum_scatter(jnp.dot(hidden, down_weight, preferred_element_type=jnp....]
    dot_general x4 -> x0, matrix products: 23.2 us -> none  [the longest x1 9 us: attend(): jnp.einsum('hemz,zhc->mhec', layer_weights, projected_values.reshape(slot...]
    all_gather x1 -> x0, waiting for transfers between devices: 17.1 us -> none  [feed_forward(): gathered = lax.all_gather(normed, 'grp', axis=0, tiled=True)]
    sub x1 -> x0, matrix products: 13.8 us -> none  [attend(): raised = jnp.exp(scores - largest)]
    all_gather x1 -> x0, blocking collectives: 13.1 us -> none  [on_device(): counts = lax.all_gather(live_rows.reshape(1), 'req', axis=0, tiled=True)]
    all_to_all x2 -> x0, starting transfers between devices: 9.9 us -> none  [the longest x1 5.52 us: on_device(): lax.all_to_all(outgoing, 'req', split_axis=1, concat_axis=1, tiled=True)]
  transfers between devices with their start and end apart: 4 -> 0, of which waited for: 4 -> 0; matrix products, arithmetic and copies ran while one was open for 0% -> 0% of each run, Pallas kernels for 0% -> 0%
where the time goes in v1:
time: 80.7 us; the launch traced here: 80.4 us
  Pallas kernels  70.7 us (88%)
  local copies, waits for them, and re-layouts  9.06 us (11%)
    pallas_call x1, Pallas kernels, on_device(): pl.pallas_call(functools.partial(kernel, blocks), out_shape=jax.ShapeDtyp...  70.7 us
    unnamed x3, local copies, waits for them, and re-layouts  6.25 us

profile of v1, /device:TPU:0, one launch (start us, length us, event | category | flops | bytes accessed | tf_op | source)
XLA Modules:
  0.0 80.4 jit_solution(1879743621462311157)
XLA Ops:
  0.7 1.3 %reshape.11.gain = f32[1,1280]{1,0:T(1,128)} reshape(f32[1280]{0:T(1024)} %param.19) | data formatting | bytes 10240 | tf_op jit(solution)/shard_map/reshape | solution.py:273
  1.9 1.5 %copy.17.seg_col = s32[512,1]{1,0:T(8,128)} copy(s32[512,1]{0,1:T(1,128)} %bitcast.2) | data formatting | bytes 4096 | tf_op jit(solution)/shard_map/reshape | solution.py:271
  3.5 1.9 %copy.15.keys = bf16[512,320]{1,0:T(8,128)(2,1)} copy(bf16[512,320]{0,1:T(8,128)(2,1)} %param.14) | data formatting | bytes 655360 | tf_op args[2]
  5.4 1.9 %copy.16.values = bf16[512,320]{1,0:T(8,128)(2,1)} copy(bf16[512,320]{0,1:T(8,128)(2,1)} %param.15) | data formatting | bytes 655360 | tf_op args[3]
  7.3 70.7 %decoder_layer.1 = bf16[512,1280]{1,0:T(8,128)(2,1)} custom-call(s32[1,1]{1,0:T(1,128)S(6)} %copy.19.live_ref, bf16[512,1280]{1,0:T(8,128)(2,1)} %queries.1, bf16[512,320]{1,0:T(8,128)(2,1)} %copy.15.keys, bf16[512,320]{1,0:T(8,128)(2,1)} %copy.16.values, s32[1,512]{1,0:T(1,128)} %bitcast.3, s32[512,1]{1,0:T(8,128)} %copy.17.seg_col, ...), custom_call_target="tpu_custom_call" | custom-call | tf_op jit(solution)/shard_map/decoder_layer/pallas_call | solution.py:236
  77.9 2.5 %copy.20 = bf16[512,1280]{1,0:T(8,128)(2,1)} copy(bf16[512,1280]{1,0:T(8,128)(2,1)} %decoder_layer.1) | data formatting | bytes 2621440

commit v2 on v1

--- a/solution.py
+++ b/solution.py
@@ -40,7 +40,8 @@
         term = exact.astype(jnp.bfloat16)
         terms.append(term)
         exact = exact - term.astype(np.float32)
-    return np.concatenate(terms, axis=1)
+    turned = np.concatenate([np.concatenate([term[:, :half], term[:, 128 : 128 + half]], axis=1).T for term in terms])
+    return np.concatenate(terms, axis=1), turned
 
 
 def dot(a, b):
@@ -53,11 +54,11 @@
 
 def kernel(
     blocks,
-    live_ref, queries, keys, values, seg_row, seg_col, table, gain, hidden_hbm, ow_hbm, gate_hbm, up_hbm, down_hbm,
+    live_ref, queries, keys, values, seg_row, table, turned_table, gain, hidden_hbm, ow_hbm, gate_hbm, up_hbm, down_hbm,
     out,
-    hidden, ow, wgu, wd, rows, context, turned_keys, wide_values, cosine, sine, mixed, act, part, own,
+    hidden, ow, wgu, wd, rows, context, turned_keys, wide_values, mixed, finished, act, part, own,
     own_out, own_in, diag_out, diag_in, across_out, across_in,
-    load_sem, send_sem, recv_sem,
+    load_sem, send_sem, recv_sem, store_sem,
 ):
     me = lax.axis_index("grp")
     sibling = me + 1 - 2 * lax.rem(me, 2)
@@ -77,12 +78,6 @@
     ow_loads = [load(ow_hbm.at[:, pl.ds(LANES * t, LANES)], ow.at[t]) for t in range(tiles)]
     ow_loads.append(load(hidden_hbm, hidden))
     ffn_loads = []
-    for t in range(hidden_tiles):
-        cols = pl.ds(HIDDEN_TILE * t, HIDDEN_TILE)
-        ffn_loads.append(load(gate_hbm.at[:, cols], wgu.at[t, :, pl.ds(0, HIDDEN_TILE)]))
-        ffn_loads.append(load(up_hbm.at[:, cols], wgu.at[t, :, pl.ds(HIDDEN_TILE, HIDDEN_TILE)]))
-    for t in range(tiles):
-        ffn_loads.append(load(down_hbm.at[:, pl.ds(LANES * t, LANES)], wd.at[t]))
 
     barrier = pltpu.get_barrier_semaphore()
     for other in (sibling, partner):
@@ -101,16 +96,19 @@
     sum_diag = [remote(SUM_DIAG, k, diag_out.at[k], diag_in.at[k], sibling) for k in range(blocks)]
     sum_across = [remote(SUM_ACROSS, k, across_out.at[k], across_in.at[k], partner) for k in range(blocks)]
 
-    same = seg_col[...] == seg_row[...]
+    ids = seg_row[...].astype(F32)
+    eye = lax.broadcasted_iota(jnp.int32, (ROWS, ROWS), 0) == lax.broadcasted_iota(jnp.int32, (ROWS, ROWS), 1)
+    id_columns = [
+        jnp.sum(jnp.where(eye, ids[:, ROWS * k : ROWS * k + ROWS], 0.0), axis=1, keepdims=True) for k in range(blocks)
+    ]
     row_ids = lax.broadcasted_iota(jnp.int32, (slots, slots), 0)
     col_ids = lax.broadcasted_iota(jnp.int32, (slots, slots), 1)
-    position = jnp.sum(jnp.where(same & (col_ids <= row_ids), 1.0, 0.0), axis=1, keepdims=True) - 1.0
-    key_position = jnp.sum(jnp.where(same & (row_ids <= col_ids), 1.0, 0.0), axis=0, keepdims=True) - 1.0
-    chosen = jnp.where(position == col_ids.astype(F32), 1.0, 0.0).astype(BF16)
-    factors = dot(chosen, table[...])
-    factors = factors[:, :256] + (factors[:, 256:512] + factors[:, 512:])
-    cosine[...] = factors[:, :128]
-    sine[...] = factors[:, 128:]
+    same = (jnp.concatenate(id_columns, axis=0) == ids) & (row_ids <= col_ids)
+    key_position = jnp.sum(jnp.where(same, 1.0, 0.0), axis=0, keepdims=True) - 1.0
+    chosen_keys = jnp.where(key_position == row_ids.astype(F32), 1.0, 0.0).astype(BF16)
+    factors = dot(turned_table[...], chosen_keys)
+    factors = factors[:64] + (factors[64:128] + factors[128:])
+    key_cos, key_sin = factors[:32], factors[32:]
 
     swap_i = lax.broadcasted_iota(jnp.int32, (256, 256), 0)
     swap_j = lax.broadcasted_iota(jnp.int32, (256, 256), 1)
@@ -118,38 +116,38 @@
     swap = jnp.where(low & (swap_i == swap_j + 32), -1.0, jnp.where(~low & (swap_i == swap_j - 32), 1.0, 0.0))
     swap = swap.astype(BF16)
 
-    key_head = keys[:, :256]
-    key_cos, key_sin = cosine[...], sine[...]
-    wide_cos = jnp.concatenate([key_cos, key_cos], axis=1)
-    wide_sin = jnp.concatenate([key_sin, key_sin], axis=1)
-    first = (key_head.astype(F32) * wide_cos + dot(key_head, swap) * wide_sin).astype(BF16)
-    key_tail = keys[:, 256:]
-    tail = (key_tail.astype(F32) * key_cos[:, :64] + dot(key_tail, swap[:64, :64]) * key_sin[:, :64]).astype(BF16)
-    ones = jnp.ones((slots, HEAD_SIZE), BF16)
+    ones = jnp.ones((HEAD_SIZE, slots), BF16)
     for n in range(KEY_VALUE_HEADS):
-        turned_keys[n] = first[:, 64 * n : 64 * n + 64] if n < 4 else tail
-        wide_values[n] = jnp.concatenate([values[:, 64 * n : 64 * n + 64], ones], axis=1)
+        first = keys[64 * n : 64 * n + 32, :].astype(F32)
+        second = keys[64 * n + 32 : 64 * n + 64, :].astype(F32)
+        turned_keys[n, :32, :] = (first * key_cos - second * key_sin).astype(BF16)
+        turned_keys[n, 32:, :] = (second * key_cos + first * key_sin).astype(BF16)
+        wide_values[n, :64, :] = values[64 * n : 64 * n + 64, :]
+        wide_values[n, 64:, :] = ones
 
     def attend(k):
         lo, width = k * ROWS, (k + 1) * ROWS
         block = pl.ds(lo, ROWS)
         q_ids = lax.broadcasted_iota(jnp.int32, (ROWS, width), 0) + lo
         k_ids = lax.broadcasted_iota(jnp.int32, (ROWS, width), 1)
-        allowed = (seg_col[block, :] == seg_row[:, :width]) & (k_ids <= q_ids)
-        allowed = allowed & ((q_ids - k_ids < WINDOW) | (key_position[:, :width] < SINK))
+        visible = (id_columns[k] == ids[:, :width]) & (k_ids <= q_ids)
+        allowed = visible & ((q_ids - k_ids < WINDOW) | (key_position[:, :width] < SINK))
         bias = jnp.where(allowed, 0.0, MASKED)
-        cos_block, sin_block = cosine[block, :], sine[block, :]
-        cos_block = jnp.concatenate([cos_block, cos_block], axis=1)
-        sin_block = jnp.concatenate([sin_block, sin_block], axis=1)
+        position = jnp.sum(jnp.where(visible, 1.0, 0.0), axis=1, keepdims=True) - 1.0
+        chosen = jnp.where(position == k_ids.astype(F32), 1.0, 0.0).astype(BF16)
+        turns = dot(chosen, table[:width, :])
+        turns = (turns[:, :256] + (turns[:, 256:512] + turns[:, 512:])) * HEAD_SIZE**-0.5
+        cos_block = jnp.concatenate([turns[:, :128], turns[:, :128]], axis=1)
+        sin_block = jnp.concatenate([turns[:, 128:], turns[:, 128:]], axis=1)
         for n in range(KEY_VALUE_HEADS):
             q = queries[block, pl.ds(256 * n, 256)]
-            q = (q.astype(F32) * cos_block + dot(q, swap) * sin_block).astype(BF16) * BF16(HEAD_SIZE**-0.5)
+            q = (q.astype(F32) * cos_block + dot(q, swap) * sin_block).astype(BF16)
             q = jnp.concatenate([q[:, 64 * h : 64 * h + 64] for h in range(HEAD_GROUP)], axis=0)
-            scores = dot_t(q, turned_keys[n, :width, :])
+            scores = dot(q, turned_keys[n, :, :width])
             scores = scores.reshape(HEAD_GROUP, ROWS, width) + bias[None]
             raised = jnp.exp(scores - jnp.max(scores, axis=-1, keepdims=True))
             raised = raised.reshape(HEAD_GROUP * ROWS, width).astype(BF16)
-            result = dot(raised, wide_values[n, :width, :])
+            result = dot_t(raised, wide_values[n, :, :width])
             result = result[:, :64] / result[:, 64:]
             context[:, 256 * n : 256 * n + 256] = jnp.concatenate(
                 [result[ROWS * h : ROWS * h + ROWS] for h in range(HEAD_GROUP)], axis=1
@@ -162,7 +160,7 @@
             mixed[block, cols] = (hidden[block, cols].astype(F32) + dot(context[...], ow[t])).astype(BF16)
         numbers = mixed[block, :].astype(F32)
         factor = lax.rsqrt(jnp.mean(numbers * numbers, axis=-1, keepdims=True) + NORM_EPS)
-        rows[k, 0] = (numbers * factor * gain[...]).astype(BF16)
+        rows[k, 0] = (numbers * factor * gain[...].reshape(1, numbers.shape[1])).astype(BF16)
 
     def feed_forward(k, first_slot):
         def upward(t, carry):
@@ -182,24 +180,26 @@
         if k == 0:
             for copy in ow_loads:
                 copy.wait()
+            for t in range(hidden_tiles):
+                cols = pl.ds(HIDDEN_TILE * t, HIDDEN_TILE)
+                ffn_loads.append(load(gate_hbm.at[:, cols], wgu.at[t, :, pl.ds(0, HIDDEN_TILE)]))
+                ffn_loads.append(load(up_hbm.at[:, cols], wgu.at[t, :, pl.ds(HIDDEN_TILE, HIDDEN_TILE)]))
+            for t in range(tiles):
+                ffn_loads.append(load(down_hbm.at[:, pl.ds(LANES * t, LANES)], wd.at[t]))
         project(k)
         if k == 0:
             pl.semaphore_wait(barrier, 2)
         to_partner[k].start()
         to_sibling[k].start()
 
-    start_block(0)
-    for k in range(blocks):
-        if k + 1 < blocks:
-            start_block(k + 1)
-        if k == 0:
-            for copy in ffn_loads:
-                copy.wait()
+    def own_rows(k):
         to_sibling[k].wait_recv()
         feed_forward(k, 0)
         own[k] = part[:ROWS, :]
         own_out[k] = part[ROWS:, :].astype(BF16)
         sum_own[k].start()
+
+    def other_rows(k):
         to_partner[k].wait_recv()
         forward[k].start()
         forward[k].wait_recv()
@@ -211,16 +211,49 @@
         sum_across[k].start()
 
     live = live_ref[0, 0]
-    for k in range(blocks):
+    stores = []
+
+    def finish(k):
         sum_own[k].wait_recv()
         sum_across[k].wait_recv()
         block = pl.ds(k * ROWS, ROWS)
         total = own[k] + own_in[k].astype(F32) + across_in[k].astype(F32) + mixed[block, :].astype(F32)
         slot = lax.broadcasted_iota(jnp.int32, total.shape, 0) + k * ROWS
-        out[block, :] = jnp.where(slot < live, total, 0.0).astype(BF16)
+        finished[block, :] = jnp.where(slot < live, total, 0.0).astype(BF16)
+        copy = pltpu.make_async_copy(finished.at[block, :], out.at[block, :], store_sem.at[k])
+        copy.start()
+        stores.append(copy)
+
+    ready = min(3, blocks)
+    for k in range(ready):
+        start_block(k)
+    for copy in ffn_loads:
+        copy.wait()
+    for k in range(blocks):
+        other_rows(k)
+        if k + ready < blocks:
+            start_block(k + ready)
+        if k >= 1:
+            own_rows(k - 1)
+    own_rows(blocks - 1)
+    for k in range(blocks):
+        finish(k)
     for k in range(blocks):
         for copy in (to_sibling[k], to_partner[k], forward[k], sum_own[k], sum_diag[k], sum_across[k]):
             copy.wait_send()
+    for copy in stores:
+        copy.wait()
+
+
+def copy_kernel(pieces, source, target, sem):
+    rows = source.shape[0] // pieces
+    copies = []
+    for n in range(pieces):
+        block = pl.ds(n * rows, rows)
+        copies.append(pltpu.make_async_copy(source.at[block, :], target.at[block, :], sem.at[n]))
+        copies[-1].start()
+    for copy in copies:
+        copy.wait()
 
 
 def on_device(
@@ -233,11 +266,12 @@
     vmem = pl.BlockSpec(memory_space=pltpu.VMEM)
     hbm = pl.BlockSpec(memory_space=pl.ANY)
     block_bf16 = pltpu.VMEM((blocks, ROWS, width), BF16)
-    return pl.pallas_call(
+    table, turned_table = rotary_table(slots)
+    result = pl.pallas_call(
         functools.partial(kernel, blocks),
         out_shape=jax.ShapeDtypeStruct((slots, width), BF16),
         in_specs=[pl.BlockSpec(memory_space=pltpu.SMEM)] + [vmem] * 7 + [hbm] * 5,
-        out_specs=vmem,
+        out_specs=hbm,
         scratch_shapes=[
             pltpu.VMEM((slots, width), BF16),
             pltpu.VMEM((tiles, width, LANES), BF16),
@@ -245,10 +279,9 @@
             pltpu.VMEM((tiles, units, LANES), BF16),
             pltpu.VMEM((blocks, 4, ROWS, width), BF16),
             pltpu.VMEM((ROWS, width), BF16),
-            pltpu.VMEM((KEY_VALUE_HEADS, slots, HEAD_SIZE), BF16),
-            pltpu.VMEM((KEY_VALUE_HEADS, slots, 2 * HEAD_SIZE), BF16),
-            pltpu.VMEM((slots, 128), F32),
-            pltpu.VMEM((slots, 128), F32),
+            pltpu.VMEM((KEY_VALUE_HEADS, HEAD_SIZE, slots), BF16),
+            pltpu.VMEM((KEY_VALUE_HEADS, 2 * HEAD_SIZE, slots), BF16),
+            pltpu.VMEM((slots, width), BF16),
             pltpu.VMEM((slots, width), BF16),
             pltpu.VMEM((hidden_tiles, 2 * ROWS, HIDDEN_TILE), BF16),
             pltpu.VMEM((2 * ROWS, width), F32),
@@ -257,6 +290,7 @@
             pltpu.SemaphoreType.DMA((2 * tiles + 2 * hidden_tiles + 1,)),
             pltpu.SemaphoreType.DMA((6, blocks)),
             pltpu.SemaphoreType.DMA((6, blocks)),
+            pltpu.SemaphoreType.DMA((blocks,)),
         ],
         compiler_params=pltpu.CompilerParams(
             collective_id=0, has_side_effects=True, vmem_limit_bytes=56 * 1024 * 1024
@@ -265,18 +299,27 @@
     )(
         live_rows,
         queries,
-        projected_keys,
-        projected_values,
+        projected_keys.T,
+        projected_values.T,
         segment.reshape(1, slots),
-        segment.reshape(slots, 1),
-        jnp.asarray(rotary_table(slots)),
-        norm_gain.reshape(1, width),
+        jnp.asarray(table),
+        jnp.asarray(turned_table),
+        norm_gain,
         hidden_in,
         out_weight,
         gate_weight,
         up_weight,
         down_weight,
     )
+    pieces = 8
+    return pl.pallas_call(
+        functools.partial(copy_kernel, pieces),
+        out_shape=jax.ShapeDtypeStruct((slots, width), BF16),
+        in_specs=[hbm],
+        out_specs=hbm,
+        scratch_shapes=[pltpu.SemaphoreType.DMA((pieces,))],
+        name="place_result",
+    )(result)
 
 
 def solution(mesh):

time: 80.7 us -> 108 us (1.34)
  Pallas kernels: 70.7 us -> 107 us
  local copies, waits for them, and re-layouts: 9.06 us -> 0 us
    pallas_call x0 -> x1, Pallas kernels: none -> 40.9 us  [on_device(): pl.pallas_call(functools.partial(copy_kernel, pieces), out_shape=jax.Shap...]
    unnamed x3 -> x0, local copies, waits for them, and re-layouts: 6.25 us -> none
    pallas_call x1, Pallas kernels: 70.7 us -> 66.4 us  [on_device(): pl.pallas_call(functools.partial(kernel, blocks), out_shape=jax.ShapeDtyp...]
    reshape x2 -> x0, local copies, waits for them, and re-layouts: 2.81 us -> none  [the longest x1 1.52 us: on_device(): segment.reshape(slots, 1)]
where the time goes in v2:
time: 108 us
  Pallas kernels  107 us (99%)
    pallas_call x1, Pallas kernels, on_device(): pl.pallas_call(functools.partial(kernel, blocks), out_shape=jax.ShapeDtyp...  66.4 us
    pallas_call x1, Pallas kernels, on_device(): pl.pallas_call(functools.partial(copy_kernel, pieces), out_shape=jax.Shap...  40.9 us

profile of v2, /device:TPU:0, one launch (start us, length us, event | category | flops | bytes accessed | tf_op | source)
XLA Modules:
  0.0 108.1 jit_solution(13461557261250594525)
XLA Ops:
  0.7 66.4 %decoder_layer.1.source = bf16[512,1280]{1,0:T(8,128)(2,1)} custom-call(s32[1,1]{1,0:T(1,128)S(6)} %copy.14.live_ref, bf16[512,1280]{1,0:T(8,128)(2,1)} %queries.1, bf16[320,512]{1,0:T(8,128)(2,1)} %bitcast.3, bf16[320,512]{1,0:T(8,128)(2,1)} %bitcast.4, s32[1,512]{1,0:T(1,128)} %bitcast.5, bf16[512,768]{1,0:T(8,128)(2,1)} %constant.4.clone.table, ...), custom_call_target="tpu_custom_call" | custom-call | tf_op jit(solution)/shard_map/decoder_layer/pallas_call | solution.py:270
  67.1 40.9 %place_result.1 = bf16[512,1280]{1,0:T(8,128)(2,1)} custom-call(bf16[512,1280]{1,0:T(8,128)(2,1)} %decoder_layer.1.source), custom_call_target="tpu_custom_call" | custom-call | tf_op jit(solution)/shard_map/place_result/pallas_call | solution.py:315

commit v3 on v2

--- a/solution.py
+++ b/solution.py
@@ -56,7 +56,7 @@
     blocks,
     live_ref, queries, keys, values, seg_row, table, turned_table, gain, hidden_hbm, ow_hbm, gate_hbm, up_hbm, down_hbm,
     out,
-    hidden, ow, wgu, wd, rows, context, turned_keys, wide_values, mixed, finished, act, part, own,
+    hidden, ow, wgu, wd, rows, context, turned_keys, wide_values, mixed, finished, act, part, own, across,
     own_out, own_in, diag_out, diag_in, across_out, across_in,
     load_sem, send_sem, recv_sem, store_sem,
 ):
@@ -199,15 +199,20 @@
         own_out[k] = part[ROWS:, :].astype(BF16)
         sum_own[k].start()
 
-    def other_rows(k):
+    def pass_on(k):
         to_partner[k].wait_recv()
         forward[k].start()
+
+    def other_rows(k):
         forward[k].wait_recv()
         feed_forward(k, 2)
         diag_out[k] = part[ROWS:, :].astype(BF16)
         sum_diag[k].start()
+        across[k] = part[:ROWS, :]
+
+    def send_across(k):
         sum_diag[k].wait_recv()
-        across_out[k] = (part[:ROWS, :] + diag_in[k].astype(F32)).astype(BF16)
+        across_out[k] = (across[k] + diag_in[k].astype(F32)).astype(BF16)
         sum_across[k].start()
 
     live = live_ref[0, 0]
@@ -227,14 +232,18 @@
     ready = min(3, blocks)
     for k in range(ready):
         start_block(k)
+    pass_on(0)
+    for k in range(ready, blocks):
+        start_block(k)
     for copy in ffn_loads:
         copy.wait()
     for k in range(blocks):
         other_rows(k)
-        if k + ready < blocks:
-            start_block(k + ready)
-        if k >= 1:
-            own_rows(k - 1)
+        if k + 1 < blocks:
+            pass_on(k + 1)
+            own_rows(k)
+            send_across(k)
+    send_across(blocks - 1)
     own_rows(blocks - 1)
     for k in range(blocks):
         finish(k)
@@ -245,15 +254,19 @@
         copy.wait()
 
 
-def copy_kernel(pieces, source, target, sem):
+def copy_kernel(pieces, source, target, held, load_sem, store_sem):
     rows = source.shape[0] // pieces
-    copies = []
+    loads, stores = [], []
     for n in range(pieces):
         block = pl.ds(n * rows, rows)
-        copies.append(pltpu.make_async_copy(source.at[block, :], target.at[block, :], sem.at[n]))
-        copies[-1].start()
-    for copy in copies:
-        copy.wait()
+        loads.append(pltpu.make_async_copy(source.at[block, :], held.at[block, :], load_sem.at[n]))
+        stores.append(pltpu.make_async_copy(held.at[block, :], target.at[block, :], store_sem.at[n]))
+        loads[-1].start()
+    for load, store in zip(loads, stores):
+        load.wait()
+        store.start()
+    for store in stores:
+        store.wait()
 
 
 def on_device(
@@ -285,6 +298,7 @@
             pltpu.VMEM((slots, width), BF16),
             pltpu.VMEM((hidden_tiles, 2 * ROWS, HIDDEN_TILE), BF16),
             pltpu.VMEM((2 * ROWS, width), F32),
+            pltpu.VMEM((blocks, ROWS, width), F32),
             pltpu.VMEM((blocks, ROWS, width), F32),
             block_bf16, block_bf16, block_bf16, block_bf16, block_bf16, block_bf16,
             pltpu.SemaphoreType.DMA((2 * tiles + 2 * hidden_tiles + 1,)),
@@ -317,7 +331,11 @@
         out_shape=jax.ShapeDtypeStruct((slots, width), BF16),
         in_specs=[hbm],
         out_specs=hbm,
-        scratch_shapes=[pltpu.SemaphoreType.DMA((pieces,))],
+        scratch_shapes=[
+            pltpu.VMEM((slots, width), BF16),
+            pltpu.SemaphoreType.DMA((pieces,)),
+            pltpu.SemaphoreType.DMA((pieces,)),
+        ],
         name="place_result",
     )(result)
 

time: 108 us -> 69.9 us (0.65)
  Pallas kernels: 107 us -> 68.9 us
    pallas_call x1, Pallas kernels: 40.9 us -> 2.21 us  [on_device(): pl.pallas_call(functools.partial(copy_kernel, pieces), out_shape=jax.Shap...]
where the time goes in v3:
time: 69.9 us; the launch traced here: 69.7 us
  Pallas kernels  68.9 us (99%)
  between operations  0.82 us (1%)
    pallas_call x1, Pallas kernels, on_device(): pl.pallas_call(functools.partial(kernel, blocks), out_shape=jax.ShapeDtyp...  66.6 us
    pallas_call x1, Pallas kernels, on_device(): pl.pallas_call(functools.partial(copy_kernel, pieces), out_shape=jax.Shap...  2.21 us

profile of v3, /device:TPU:0, one launch (start us, length us, event | category | flops | bytes accessed | tf_op | source)
XLA Modules:
  0.0 69.7 jit_solution(18153493810987889603)
XLA Ops:
  0.7 66.6 %decoder_layer.1.source = bf16[512,1280]{1,0:T(8,128)(2,1)} custom-call(s32[1,1]{1,0:T(1,128)S(6)} %copy.14.live_ref, bf16[512,1280]{1,0:T(8,128)(2,1)} %queries.1, bf16[320,512]{1,0:T(8,128)(2,1)} %bitcast.3, bf16[320,512]{1,0:T(8,128)(2,1)} %bitcast.4, s32[1,512]{1,0:T(1,128)} %bitcast.5, bf16[512,768]{1,0:T(8,128)(2,1)} %constant.4.clone.table, ...), custom_call_target="tpu_custom_call" | custom-call | tf_op jit(solution)/shard_map/decoder_layer/pallas_call | solution.py:283
  67.3 2.2 %place_result.1 = bf16[512,1280]{1,0:T(8,128)(2,1)} custom-call(bf16[512,1280]{1,0:T(8,128)(2,1)} %decoder_layer.1.source), custom_call_target="tpu_custom_call" | custom-call | tf_op jit(solution)/shard_map/place_result/pallas_call | solution.py:329

commit v4 on v3

--- a/solution.py
+++ b/solution.py
@@ -101,37 +101,43 @@
     id_columns = [
         jnp.sum(jnp.where(eye, ids[:, ROWS * k : ROWS * k + ROWS], 0.0), axis=1, keepdims=True) for k in range(blocks)
     ]
-    row_ids = lax.broadcasted_iota(jnp.int32, (slots, slots), 0)
-    col_ids = lax.broadcasted_iota(jnp.int32, (slots, slots), 1)
-    same = (jnp.concatenate(id_columns, axis=0) == ids) & (row_ids <= col_ids)
-    key_position = jnp.sum(jnp.where(same, 1.0, 0.0), axis=0, keepdims=True) - 1.0
-    chosen_keys = jnp.where(key_position == row_ids.astype(F32), 1.0, 0.0).astype(BF16)
-    factors = dot(turned_table[...], chosen_keys)
-    factors = factors[:64] + (factors[64:128] + factors[128:])
-    key_cos, key_sin = factors[:32], factors[32:]
-
     swap_i = lax.broadcasted_iota(jnp.int32, (256, 256), 0)
     swap_j = lax.broadcasted_iota(jnp.int32, (256, 256), 1)
     low = lax.rem(swap_j, HEAD_SIZE) < HEAD_SIZE // 2
     swap = jnp.where(low & (swap_i == swap_j + 32), -1.0, jnp.where(~low & (swap_i == swap_j - 32), 1.0, 0.0))
     swap = swap.astype(BF16)
 
-    ones = jnp.ones((HEAD_SIZE, slots), BF16)
-    for n in range(KEY_VALUE_HEADS):
-        first = keys[64 * n : 64 * n + 32, :].astype(F32)
-        second = keys[64 * n + 32 : 64 * n + 64, :].astype(F32)
-        turned_keys[n, :32, :] = (first * key_cos - second * key_sin).astype(BF16)
-        turned_keys[n, 32:, :] = (second * key_cos + first * key_sin).astype(BF16)
-        wide_values[n, :64, :] = values[64 * n : 64 * n + 64, :]
-        wide_values[n, 64:, :] = ones
+    ones = jnp.ones((HEAD_SIZE, ROWS), BF16)
+    key_positions = []
+
+    def prepare(k):
+        lo, width = k * ROWS, (k + 1) * ROWS
+        block = pl.ds(lo, ROWS)
+        row_ids = lax.broadcasted_iota(jnp.int32, (width, ROWS), 0)
+        col_ids = lax.broadcasted_iota(jnp.int32, (width, ROWS), 1) + lo
+        same = (jnp.concatenate(id_columns[: k + 1], axis=0) == ids[:, lo:width]) & (row_ids <= col_ids)
+        key_position = jnp.sum(jnp.where(same, 1.0, 0.0), axis=0, keepdims=True) - 1.0
+        key_positions.append(key_position)
+        chosen_keys = jnp.where(key_position == row_ids.astype(F32), 1.0, 0.0).astype(BF16)
+        factors = dot(turned_table[:, :width], chosen_keys)
+        factors = factors[:64] + (factors[64:128] + factors[128:])
+        key_cos, key_sin = factors[:32], factors[32:]
+        for n in range(KEY_VALUE_HEADS):
+            first = keys[64 * n : 64 * n + 32, block].astype(F32)
+            second = keys[64 * n + 32 : 64 * n + 64, block].astype(F32)
+            turned_keys[n, :32, block] = (first * key_cos - second * key_sin).astype(BF16)
+            turned_keys[n, 32:, block] = (second * key_cos + first * key_sin).astype(BF16)
+            wide_values[n, :64, block] = values[64 * n : 64 * n + 64, block]
+            wide_values[n, 64:, block] = ones
 
     def attend(k):
         lo, width = k * ROWS, (k + 1) * ROWS
         block = pl.ds(lo, ROWS)
         q_ids = lax.broadcasted_iota(jnp.int32, (ROWS, width), 0) + lo
         k_ids = lax.broadcasted_iota(jnp.int32, (ROWS, width), 1)
+        key_position = jnp.concatenate(key_positions, axis=1)
         visible = (id_columns[k] == ids[:, :width]) & (k_ids <= q_ids)
-        allowed = visible & ((q_ids - k_ids < WINDOW) | (key_position[:, :width] < SINK))
+        allowed = visible & ((q_ids - k_ids < WINDOW) | (key_position < SINK))
         bias = jnp.where(allowed, 0.0, MASKED)
         position = jnp.sum(jnp.where(visible, 1.0, 0.0), axis=1, keepdims=True) - 1.0
         chosen = jnp.where(position == k_ids.astype(F32), 1.0, 0.0).astype(BF16)
@@ -176,6 +182,7 @@
             part[:, LANES * t : LANES * t + LANES] = dot(hid, wd[t])
 
     def start_block(k):
+        prepare(k)
         attend(k)
         if k == 0:
             for copy in ow_loads:
@@ -241,10 +248,12 @@
         other_rows(k)
         if k + 1 < blocks:
             pass_on(k + 1)
-            own_rows(k)
-            send_across(k)
+        if k >= 1:
+            send_across(k - 1)
+    own_rows(0)
     send_across(blocks - 1)
-    own_rows(blocks - 1)
+    for k in range(1, blocks):
+        own_rows(k)
     for k in range(blocks):
         finish(k)
     for k in range(blocks):

time: 69.9 us -> 69.7 us (level)
  no operation moved by 1% of the time
where the time goes in v4:
time: 69.7 us; the launch traced here: 69.5 us
  Pallas kernels  68.7 us (99%)
  between operations  0.82 us (1%)
    pallas_call x1, Pallas kernels, on_device(): pl.pallas_call(functools.partial(kernel, blocks), out_shape=jax.ShapeDtyp...  66.5 us
    pallas_call x1, Pallas kernels, on_device(): pl.pallas_call(functools.partial(copy_kernel, pieces), out_shape=jax.Shap...  2.21 us

profile of v4, /device:TPU:0, one launch (start us, length us, event | category | flops | bytes accessed | tf_op | source)
XLA Modules:
  0.0 69.5 jit_solution(3017607935750565966)
XLA Ops:
  0.7 66.5 %decoder_layer.1.source = bf16[512,1280]{1,0:T(8,128)(2,1)} custom-call(s32[1,1]{1,0:T(1,128)S(6)} %copy.14.live_ref, bf16[512,1280]{1,0:T(8,128)(2,1)} %queries.1, bf16[320,512]{1,0:T(8,128)(2,1)} %bitcast.3, bf16[320,512]{1,0:T(8,128)(2,1)} %bitcast.4, s32[1,512]{1,0:T(1,128)} %bitcast.5, bf16[512,768]{1,0:T(8,128)(2,1)} %constant.4.clone.table, ...), custom_call_target="tpu_custom_call" | custom-call | tf_op jit(solution)/shard_map/decoder_layer/pallas_call | solution.py:292
  67.1 2.2 %place_result.1 = bf16[512,1280]{1,0:T(8,128)(2,1)} custom-call(bf16[512,1280]{1,0:T(8,128)(2,1)} %decoder_layer.1.source), custom_call_target="tpu_custom_call" | custom-call | tf_op jit(solution)/shard_map/place_result/pallas_call | solution.py:338

commit v5 on v4

--- a/solution.py
+++ b/solution.py
@@ -170,13 +170,13 @@
 
     def feed_forward(k, first_slot):
         def upward(t, carry):
-            both = rows[k, first_slot : first_slot + 2].reshape(2 * ROWS, rows.shape[3])
+            both = rows[k : k + 2, first_slot : first_slot + 2].reshape(4 * ROWS, rows.shape[3])
             product = dot(both, wgu[t])
             gate, up = product[:, :HIDDEN_TILE], product[:, HIDDEN_TILE:]
             act[t] = (gate / (1.0 + jnp.exp(-gate)) * up).astype(BF16)
             return carry
 
-        lax.fori_loop(0, hidden_tiles, upward, 0)
+        lax.fori_loop(0, hidden_tiles, upward, 0, unroll=True)
         for t in range(tiles):
             hid = jnp.concatenate([act[j] for j in range(hidden_tiles)], axis=1)
             part[:, LANES * t : LANES * t + LANES] = dot(hid, wd[t])
@@ -199,23 +199,27 @@
         to_partner[k].start()
         to_sibling[k].start()
 
-    def own_rows(k):
-        to_sibling[k].wait_recv()
-        feed_forward(k, 0)
-        own[k] = part[:ROWS, :]
-        own_out[k] = part[ROWS:, :].astype(BF16)
-        sum_own[k].start()
+    def own_rows(pair):
+        for k in pair:
+            to_sibling[k].wait_recv()
+        feed_forward(pair[0], 0)
+        for j, k in enumerate(pair):
+            own[k] = part[2 * j * ROWS : (2 * j + 1) * ROWS, :]
+            own_out[k] = part[(2 * j + 1) * ROWS : (2 * j + 2) * ROWS, :].astype(BF16)
+            sum_own[k].start()
 
     def pass_on(k):
         to_partner[k].wait_recv()
         forward[k].start()
 
-    def other_rows(k):
-        forward[k].wait_recv()
-        feed_forward(k, 2)
-        diag_out[k] = part[ROWS:, :].astype(BF16)
-        sum_diag[k].start()
-        across[k] = part[:ROWS, :]
+    def other_rows(pair):
+        for k in pair:
+            forward[k].wait_recv()
+        feed_forward(pair[0], 2)
+        for j, k in enumerate(pair):
+            diag_out[k] = part[(2 * j + 1) * ROWS : (2 * j + 2) * ROWS, :].astype(BF16)
+            sum_diag[k].start()
+            across[k] = part[2 * j * ROWS : (2 * j + 1) * ROWS, :]
 
     def send_across(k):
         sum_diag[k].wait_recv()
@@ -236,24 +240,24 @@
         copy.start()
         stores.append(copy)
 
-    ready = min(3, blocks)
-    for k in range(ready):
+    for k in range(blocks - 1):
         start_block(k)
     pass_on(0)
-    for k in range(ready, blocks):
-        start_block(k)
+    start_block(blocks - 1)
+    pass_on(1)
     for copy in ffn_loads:
         copy.wait()
-    for k in range(blocks):
-        other_rows(k)
-        if k + 1 < blocks:
-            pass_on(k + 1)
-        if k >= 1:
-            send_across(k - 1)
-    own_rows(0)
-    send_across(blocks - 1)
-    for k in range(1, blocks):
-        own_rows(k)
+    for first in range(0, blocks, 2):
+        pair = (first, first + 1)
+        other_rows(pair)
+        if first + 2 < blocks:
+            pass_on(first + 2)
+        for k in pair:
+            send_across(k)
+        if first + 2 < blocks:
+            own_rows(pair)
+            pass_on(first + 3)
+    own_rows((blocks - 2, blocks - 1))
     for k in range(blocks):
         finish(k)
     for k in range(blocks):
@@ -305,8 +309,8 @@
             pltpu.VMEM((KEY_VALUE_HEADS, 2 * HEAD_SIZE, slots), BF16),
             pltpu.VMEM((slots, width), BF16),
             pltpu.VMEM((slots, width), BF16),
-            pltpu.VMEM((hidden_tiles, 2 * ROWS, HIDDEN_TILE), BF16),
-            pltpu.VMEM((2 * ROWS, width), F32),
+            pltpu.VMEM((hidden_tiles, 4 * ROWS, HIDDEN_TILE), BF16),
+            pltpu.VMEM((4 * ROWS, width), F32),
             pltpu.VMEM((blocks, ROWS, width), F32),
             pltpu.VMEM((blocks, ROWS, width), F32),
             block_bf16, block_bf16, block_bf16, block_bf16, block_bf16, block_bf16,

time: 69.7 us -> 69.7 us (level)
  no operation moved by 1% of the time
where the time goes in v5:
time: 69.7 us; the launch traced here: 69.5 us
  Pallas kernels  68.6 us (98%)
  between operations  0.82 us (1%)
    pallas_call x1, Pallas kernels, on_device(): pl.pallas_call(functools.partial(kernel, blocks), out_shape=jax.ShapeDtyp...  66.4 us
    pallas_call x1, Pallas kernels, on_device(): pl.pallas_call(functools.partial(copy_kernel, pieces), out_shape=jax.Shap...  2.21 us

profile of v5, /device:TPU:0, one launch (start us, length us, event | category | flops | bytes accessed | tf_op | source)
XLA Modules:
  0.0 69.5 jit_solution(2166863616176789250)
XLA Ops:
  0.7 66.4 %decoder_layer.1.source = bf16[512,1280]{1,0:T(8,128)(2,1)} custom-call(s32[1,1]{1,0:T(1,128)S(6)} %copy.14.live_ref, bf16[512,1280]{1,0:T(8,128)(2,1)} %queries.1, bf16[320,512]{1,0:T(8,128)(2,1)} %bitcast.3, bf16[320,512]{1,0:T(8,128)(2,1)} %bitcast.4, s32[1,512]{1,0:T(1,128)} %bitcast.5, bf16[512,768]{1,0:T(8,128)(2,1)} %constant.4.clone.table, ...), custom_call_target="tpu_custom_call" | custom-call | tf_op jit(solution)/shard_map/decoder_layer/pallas_call | solution.py:296
  67.1 2.2 %place_result.1 = bf16[512,1280]{1,0:T(8,128)(2,1)} custom-call(bf16[512,1280]{1,0:T(8,128)(2,1)} %decoder_layer.1.source), custom_call_target="tpu_custom_call" | custom-call | tf_op jit(solution)/shard_map/place_result/pallas_call | solution.py:342
